TPU v7x, 256 devices: a whole 4x4x8 slice. The times are simulated.
256 devices in a mesh: rows: 16 (over z_hi, x), cols: 4 (over z_lo, core), depth: 4 (over y).
Axes of the slice: x: 4, y: 4, z: 8 (z_hi: 4, z_lo: 2; z = z_hi * 2 + z_lo), core: 2. Of those that a mesh axis runs over, the one named last changes fastest.
Arguments:
- tokens_in: bfloat16 [256, 8192], P('rows', 'depth'), may hold values from -6 to 6
- cotangent: bfloat16 [256, 8192], P('rows', 'depth'), may hold values from -1.5 to 1.5
- w_gate: bfloat16 [8192, 28672], P('depth', ('rows', 'cols')), may hold values from -0.0625 to 0.0625
- w_up: bfloat16 [8192, 28672], P('depth', ('rows', 'cols')), may hold values from -0.0625 to 0.0625
- w_down: bfloat16 [28672, 8192], P(('rows', 'cols'), 'depth'), may hold values from -0.03125 to 0.03125
Outputs:
- block_out: bfloat16 [256, 8192], P(('rows', 'cols'), 'depth')
- input_grad: bfloat16 [256, 8192], P(('rows', 'cols'), 'depth')
- gate_grad: bfloat16 [8192, 28672], P('depth', ('rows', 'cols'))
- up_grad: bfloat16 [8192, 28672], P('depth', ('rows', 'cols'))
- down_grad: bfloat16 [28672, 8192], P(('rows', 'cols'), 'depth')
All inputs are finite; a program needn't handle non-finite values.
Results may differ from a plain program's by a relative error of at most 0.0049.
Values may be sent and summed in bfloat16 or wider, within the bound.
A program may use at most 64 MiB of HBM per device.

v0:
```python
import jax
import jax.numpy as jnp
from jax import lax
from jax.sharding import PartitionSpec as P


def backward_local(hidden_back, gate, up):
    sigma = jax.nn.sigmoid(gate)
    up_back = (hidden_back * gate * sigma).astype(jnp.bfloat16)
    gate_back = (hidden_back * up * sigma * (1.0 + gate * (1.0 - sigma))).astype(jnp.bfloat16)
    return (gate_back, up_back)


def contract_last(left, right):
    return lax.dot_general(
        left, right, (((1,), (1,)), ((), ())), preferred_element_type=jnp.float32
    )


def contract_first(left, right):
    return lax.dot_general(
        left, right, (((0,), (0,)), ((), ())), preferred_element_type=jnp.float32
    )


def on_device(tokens_in, cotangent, w_gate, w_up, w_down):
    tokens_full, cotangent_full = (
        lax.all_gather(tokens_in, "rows", axis=0, tiled=True),
        lax.all_gather(cotangent, "rows", axis=0, tiled=True),
    )
    gate_part = jnp.dot(tokens_full, w_gate, preferred_element_type=jnp.float32)
    up_part = jnp.dot(tokens_full, w_up, preferred_element_type=jnp.float32)
    gate, up = lax.psum((gate_part, up_part), "depth")
    hidden = (jax.nn.silu(gate) * up).astype(jnp.bfloat16)
    output_sum = lax.psum_scatter(
        jnp.dot(hidden, w_down, preferred_element_type=jnp.float32),
        ("rows", "cols"),
        scatter_dimension=0,
        tiled=True,
    )
    block_out = output_sum.astype(jnp.bfloat16)
    back_part = contract_last(cotangent_full, w_down)
    hidden_back = lax.psum(back_part, "depth")
    gate_back, up_back = backward_local(hidden_back, gate, up)
    input_grad = lax.psum_scatter(
        contract_last(gate_back, w_gate) + contract_last(up_back, w_up),
        ("rows", "cols"),
        scatter_dimension=0,
        tiled=True,
    ).astype(jnp.bfloat16)
    gate_grad = contract_first(tokens_full, gate_back).astype(jnp.bfloat16)
    up_grad = contract_first(tokens_full, up_back).astype(jnp.bfloat16)
    down_grad = contract_first(hidden, cotangent_full).astype(jnp.bfloat16)
    return (block_out, input_grad, gate_grad, up_grad, down_grad)


def solution(mesh):
    return jax.shard_map(
        on_device,
        mesh=mesh,
        in_specs=(
            P("rows", "depth"),
            P("rows", "depth"),
            P("depth", ("rows", "cols")),
            P("depth", ("rows", "cols")),
            P(("rows", "cols"), "depth"),
        ),
        out_specs=(
            P(("rows", "cols"), "depth"),
            P(("rows", "cols"), "depth"),
            P("depth", ("rows", "cols")),
            P("depth", ("rows", "cols")),
            P(("rows", "cols"), "depth"),
        ),
        check_vma=False,
    )
```

profile of v0, /device:TPU:8, one launch (start us, length us, event | category | flops | bytes accessed | tf_op | source)
XLA Modules:
  0.0 490.9 jit_solution(15707571623628139926)
XLA Ops:
  7.2 0.0 copy-start
  7.2 0.0 all-gather.3.cloned.1.call-start
  7.2 0.7 all-gather.3.cloned.1.call-update
  7.9 0.0 all-gather.5.cloned.1.call-start
  8.0 0.7 all-gather.5.cloned.1.call-update
  8.7 0.0 all-reduce.7.cloned.1.call-start
  8.7 58.4 %all-gather.3.cloned.1.call-done = bf16[256,2048]{1,0:T(8,128)(2,1)} async-done(((bf16[16,2048]{1,0:T(8,128)(2,1)}), bf16[256,2048]{1,0:T(8,128)(2,1)}) %all-gather.3.cloned.1.call-update) | async-done | bytes 1048592 | tf_op jit(solution)/shard_map/all_gather | solution.py:28
  67.1 0.0 copy-done
  67.1 2.8 fusion.2
  69.9 0.0 copy-done.1
  69.9 0.0 copy-done.2
  69.9 1.4 fusion.3
  71.4 48.9 %all-gather.5.cloned.1.call-done = bf16[256,2048]{1,0:T(8,128)(2,1)} async-done(((bf16[16,2048]{1,0:T(8,128)(2,1)}), bf16[256,2048]{1,0:T(8,128)(2,1)}) %all-gather.5.cloned.1.call-update) | async-done | bytes 1048592 | tf_op jit(solution)/shard_map/all_gather | solution.py:29
  120.3 3.3 fusion.5
  123.6 0.0 all-reduce.7.cloned.1.call-update
  123.6 0.0 copy-done.7
  123.6 0.6 dynamic-slice
  124.9 48.7 %all-reduce.7.cloned.1.call-done = (f32[256,448]{0,1:T(8,128)}, f32[256,448]{0,1:T(8,128)}, f32[256,448]{0,1:T(8,128)}) async-done(((f32[256,448]{0,1:T(8,128)}, f32[256,448]{0,1:T(8,128)}, f32[256,448]{0,1:T(8,128)}), (f32[256,448]{0,1:T(8,128)}, f32[256,448]{0,1:T(8,128)}, f32[256,448]{0,1:T(8,128)})) %all-reduce.7.cloned.1.call-update) | async-done | bytes 1376272 | tf_op jit(solution)/shard_map/psum | solution.py:33
  173.6 1.5 multiply_convert_fusion
  175.1 0.0 copy-start.6
  175.1 0.0 copy-start.3
  175.1 0.7 fusion.6
  175.9 0.0 copy-done.6
  175.9 0.8 copy-done.3
  176.7 2.1 convolution_add_fusion
  178.8 2.1 fusion.4
  180.8 295.6 %all-reduce.8 = (bf16[256,2048]{1,0:T(8,128)(2,1)}, bf16[256,2048]{1,0:T(8,128)(2,1)}) all-reduce(f32[256,2048]{1,0:T(8,128)} %fusion.4, f32[256,2048]{1,0:T(8,128)} %convolution_add_fusion), channel_id=2, replica_groups=mesh['rows'=16,'cols'=4,'depth'=4] {'rows','cols'}, use_global_device_ids=true, to_apply=%region_2.3.clone | all-reduce | flops 1048576 | bytes 6291456
  476.4 1.4 dynamic-slice_convert_fusion
  477.8 2.8 fusion
  480.6 1.9 fusion.1
  482.5 0.0 copy-done.5
  482.5 1.9 convolution_convert_fusion
  (6 shorter events, 0.0 us)
Async XLA Ops:
  7.2 60.0 %copy-start = (bf16[2048,448]{0,1:T(8,128)(2,1)S(1)}, bf16[2048,448]{0,1:T(8,128)(2,1)}, u32[]{:S(2)}) copy-start(bf16[2048,448]{0,1:T(8,128)(2,1)} %param.7) | copy-start | bytes 5505028
  7.2 59.9 %all-gather.3.cloned.1.call-start = ((), (), s32[]{:S(2)}) async-start(), calls=%async_computation | async-start | bytes 1114112 | tf_op jit(solution)/shard_map/all_gather | solution.py:28
  7.9 112.4 %all-gather.5.cloned.1.call-start = ((), (), s32[]{:S(2)}) async-start(), calls=%async_computation.1 | async-start | bytes 1114112 | tf_op jit(solution)/shard_map/all_gather | solution.py:29
  8.7 164.9 %all-reduce.7.cloned.1.call-start = ((), (), s32[]{:S(2)}) async-start(), calls=%async_computation.2 | async-start | bytes 2752512 | tf_op jit(solution)/shard_map/psum | solution.py:33
  67.1 2.8 copy-start.1
  67.1 2.8 copy-start.2
  71.4 52.2 %copy-start.7 = (u32[256]{0:T(256)S(1)}, u32[256]{0:T(256)}, u32[]{:S(2)}) copy-start(u32[256]{0:T(256)} %constant.6) | copy-start | bytes 3076
  175.1 0.8 copy-start.6
  175.1 1.6 copy-start.3
  176.7 2.1 copy-start.4
  480.6 1.9 copy-start.5
Sparse Core Ops, SparseCore 0:
  10.4 56.6 all-gather.2
  69.5 50.7 all-gather.4
  123.7 49.7 all-reduce.6
where the time goes:
time: 491 us
  blocking collectives  296 us (60%)
  waiting for transfers between devices  157 us (32%)
  matrix products  18.9 us (4%)
  between operations  14.5 us (3%)
    unnamed x1, blocking collectives  296 us
    all_gather x1, waiting for transfers between devices, on_device(): lax.all_gather(tokens_in, 'rows', axis=0, tiled=True)  58.4 us
    all_gather x1, waiting for transfers between devices, on_device(): lax.all_gather(cotangent, 'rows', axis=0, tiled=True)  48.9 us
    psum x1, waiting for transfers between devices, on_device(): gate, up = lax.psum((gate_part, up_part), 'depth')  48.7 us
  transfers between devices with their start and end apart: 3, of which 3 were waited for; matrix products, arithmetic and copies ran while one was open for 1% of the time, Pallas kernels for 0%

commit v1 on v0

--- a/solution.py
+++ b/solution.py
@@ -25,7 +25,9 @@
 
 def on_device(tokens_in, cotangent, w_gate, w_up, w_down):
     tokens_full, cotangent_full = (
-        lax.all_gather(tokens_in, "rows", axis=0, tiled=True),
+        jnp.concatenate(
+            lax.all_to_all(jnp.stack([tokens_in] * lax.axis_size("rows")), "rows", 0, 0), axis=0
+        ),
         lax.all_gather(cotangent, "rows", axis=0, tiled=True),
     )
     gate_part = jnp.dot(tokens_full, w_gate, preferred_element_type=jnp.float32)

time: 491 us -> 452 us (0.921)
  waiting for transfers between devices: 157 us -> 107 us
  starting transfers between devices: 0.11 us -> 11.1 us
    all_gather x1 -> x0, waiting for transfers between devices: 58.4 us -> none  [on_device(): lax.all_gather(tokens_in, 'rows', axis=0, tiled=True)]
    all_to_all x0 -> x1, waiting for transfers between devices: none -> 28 us  [on_device(): lax.all_to_all(jnp.stack([tokens_in] * lax.axis_size('rows')), 'rows', 0, 0)]
    all_gather x1, waiting for transfers between devices: 48.9 us -> 30 us  [on_device(): lax.all_gather(cotangent, 'rows', axis=0, tiled=True)]
    all_to_all x0 -> x1, starting transfers between devices: none -> 11 us  [on_device(): lax.all_to_all(jnp.stack([tokens_in] * lax.axis_size('rows')), 'rows', 0, 0)]
where the time goes in v1:
time: 452 us; the launch traced here: 451 us
  blocking collectives  296 us (65%)
  waiting for transfers between devices  107 us (24%)
  matrix products  16.6 us (4%)
  between operations  14.7 us (3%)
  starting transfers between devices  11.1 us (2%)
    unnamed x1, blocking collectives  296 us
    psum x1, waiting for transfers between devices, on_device(): gate, up = lax.psum((gate_part, up_part), 'depth')  48.7 us
    all_gather x1, waiting for transfers between devices, on_device(): lax.all_gather(cotangent, 'rows', axis=0, tiled=True)  30 us
    all_to_all x1, waiting for transfers between devices, on_device(): lax.all_to_all(jnp.stack([tokens_in] * lax.axis_size('rows')), 'rows', 0, 0)  28 us
    all_to_all x1, starting transfers between devices, on_device(): lax.all_to_all(jnp.stack([tokens_in] * lax.axis_size('rows')), 'rows', 0, 0)  11 us
  transfers between devices with their start and end apart: 3, of which 3 were waited for; matrix products, arithmetic and copies ran while one was open for 1% of the time, Pallas kernels for 0%

profile of v1, /device:TPU:8, one launch (start us, length us, event | category | flops | bytes accessed | tf_op | source)
XLA Modules:
  0.0 451.3 jit_solution(7450210718069729126)
XLA Ops:
  7.2 0.0 copy-start
  7.2 2.1 stack.2
  9.2 11.0 %all-to-all-start = ((bf16[16,16,2048]{2,1,0:T(8,128)(2,1)}), bf16[16,16,2048]{2,1,0:T(8,128)(2,1)S(1)}, u32[]{:S(2)}, u32[]{:S(2)}) async-start(bf16[16,16,2048]{2,1,0:T(8,128)(2,1)} %stack.2), calls=%async_computation | async-start | bytes 2097152 | tf_op jit(solution)/shard_map/all_to_all | solution.py:29
  20.3 0.0 all-gather.2.cloned.1.call-start
  20.3 0.7 all-gather.2.cloned.1.call-update
  21.0 0.0 all-reduce.7.cloned.1.call-start
  21.1 28.0 %all-to-all-done = bf16[16,16,2048]{2,1,0:T(8,128)(2,1)S(1)} async-done(((bf16[16,16,2048]{2,1,0:T(8,128)(2,1)}), bf16[16,16,2048]{2,1,0:T(8,128)(2,1)S(1)}, u32[]{:S(2)}, u32[]{:S(2)}) %all-to-all-start) | async-done | bytes 1048608 | tf_op jit(solution)/shard_map/all_to_all | solution.py:29
  49.0 0.0 copy-start.1
  49.0 0.0 copy-done
  49.0 1.4 fusion.2
  50.5 0.1 copy-done.1
  50.5 1.4 fusion.3
  52.0 0.0 copy-start.5
  52.0 30.0 %all-gather.2.cloned.1.call-done = bf16[256,2048]{1,0:T(8,128)(2,1)} async-done(((bf16[16,2048]{1,0:T(8,128)(2,1)}), bf16[256,2048]{1,0:T(8,128)(2,1)}) %all-gather.2.cloned.1.call-update) | async-done | bytes 1048592 | tf_op jit(solution)/shard_map/all_gather | solution.py:31
  82.0 3.3 fusion.5
  85.3 0.0 all-reduce.7.cloned.1.call-update
  85.3 0.0 copy-done.5
  85.3 0.6 dynamic-slice
  86.6 48.7 %all-reduce.7.cloned.1.call-done = (f32[256,448]{0,1:T(8,128)}, f32[256,448]{0,1:T(8,128)}, f32[256,448]{0,1:T(8,128)}) async-done(((f32[256,448]{0,1:T(8,128)}, f32[256,448]{0,1:T(8,128)}, f32[256,448]{0,1:T(8,128)}), (f32[256,448]{0,1:T(8,128)}, f32[256,448]{0,1:T(8,128)}, f32[256,448]{0,1:T(8,128)})) %all-reduce.7.cloned.1.call-update) | async-done | bytes 1376272 | tf_op jit(solution)/shard_map/psum | solution.py:35
  135.3 1.5 multiply_convert_fusion
  136.8 0.7 fusion.6
  137.6 1.9 fusion
  139.4 0.0 copy-start.2
  139.4 1.9 fusion.1
  141.3 0.0 copy-done.2
  141.3 2.0 convolution_add_fusion
  143.4 0.0 copy-done.3
  143.4 2.1 fusion.4
  145.4 295.7 %all-reduce.8 = (bf16[256,2048]{1,0:T(8,128)(2,1)}, bf16[256,2048]{1,0:T(8,128)(2,1)}) all-reduce(f32[256,2048]{1,0:T(8,128)} %fusion.4, f32[256,2048]{1,0:T(8,128)} %convolution_add_fusion), channel_id=2, replica_groups=mesh['rows'=16,'cols'=4,'depth'=4] {'rows','cols'}, use_global_device_ids=true, to_apply=%region_2.3.clone | all-reduce | flops 1048576 | bytes 6291456
  441.1 1.4 dynamic-slice_convert_fusion
  442.5 0.0 copy-done.4
  442.5 1.9 convolution_convert_fusion
  (2 shorter events, 0.0 us)
Async XLA Ops:
  7.2 41.9 %copy-start = (bf16[2048,448]{0,1:T(8,128)(2,1)S(1)}, bf16[2048,448]{0,1:T(8,128)(2,1)}, u32[]{:S(2)}) copy-start(bf16[2048,448]{0,1:T(8,128)(2,1)} %param.7) | copy-start | bytes 5505028
  9.2 39.8 %all-to-all-start = ((bf16[16,16,2048]{2,1,0:T(8,128)(2,1)}), bf16[16,16,2048]{2,1,0:T(8,128)(2,1)S(1)}, u32[]{:S(2)}, u32[]{:S(2)}) async-start(bf16[16,16,2048]{2,1,0:T(8,128)(2,1)} %stack.2), calls=%async_computation | async-start | bytes 2097152 | tf_op jit(solution)/shard_map/all_to_all | solution.py:29
  20.3 61.7 %all-gather.2.cloned.1.call-start = ((), (), s32[]{:S(2)}) async-start(), calls=%async_computation.1 | async-start | bytes 1114112 | tf_op jit(solution)/shard_map/all_gather | solution.py:31
  21.0 114.3 %all-reduce.7.cloned.1.call-start = ((), (), s32[]{:S(2)}) async-start(), calls=%async_computation.2 | async-start | bytes 2752512 | tf_op jit(solution)/shard_map/psum | solution.py:35
  49.0 1.5 copy-start.1
  52.0 33.3 %copy-start.5 = (u32[256]{0:T(256)S(1)}, u32[256]{0:T(256)}, u32[]{:S(2)}) copy-start(u32[256]{0:T(256)} %constant.6) | copy-start | bytes 3076
  139.4 1.9 copy-start.2
  141.3 2.0 copy-start.3
  145.4 297.1 %copy-start.4 = (bf16[256,2048]{1,0:T(8,128)(2,1)S(1)}, bf16[256,2048]{1,0:T(8,128)(2,1)}, u32[]{:S(2)}) copy-start(bf16[256,2048]{1,0:T(8,128)(2,1)} %all-gather.2.cloned.1.call-done) | copy-start | bytes 3145732
Sparse Core Ops, SparseCore 0:
  23.6 58.4 all-gather.1
  85.4 49.8 all-reduce.6
